TPU v7x, 32 devices: a whole 2x2x4 slice. The times are simulated.
32 devices in a mesh: expert: 4 (over z), tensor: 8 (over y, x, core).
Axes of the slice: x: 2, y: 2, z: 4, core: 2. Of those that a mesh axis runs over, the one named last changes fastest.
Arguments:
- activations: bfloat16 [3072, 512], P('tensor', 'expert'), may hold values from -6 to 6
- cotangent: bfloat16 [3072, 512], P('tensor', 'expert'), may hold values from -4 to 4
- route_ids: int32 [512, 2], P('expert'), may hold values from 0 to 3, all different within a row; in each aligned block of 128 rows (0 to 127, 128 to 255, ...) at most 80 rows name the same one
- gate_probs: float32 [512, 2], P('expert'), may hold values from 0.2 to 0.8
- gate_weight: bfloat16 [4, 3072, 16384], P('expert', None, 'tensor'), may hold values from -0.15625 to 0.15625
- up_weight: bfloat16 [4, 3072, 16384], P('expert', None, 'tensor'), may hold values from -0.15625 to 0.15625
- down_weight: bfloat16 [4, 16384, 3072], P('expert', 'tensor'), may hold values from -0.046875 to 0.046875
Outputs:
- grad_input: bfloat16 [3072, 512], P('tensor', 'expert')
- score_grad: float32 [512, 2], P('expert')
Inputs may be any that keep to these rules, and one draw needn't show every extreme that they name: `route_ids`: each token names 2 different experts. Among the 128 tokens of one index of the expert axis no expert is named more than 80 times, and in every draw some such block names one expert exactly 80 times.
All inputs are finite; a program needn't handle non-finite values.
Results may differ from a plain program's by a relative error of at most 0.008.
Values may be sent and summed in bfloat16 or wider, within the bound.
A program may use at most 128 MiB of HBM per device.

v0:
```python
import jax
import jax.numpy as jnp
from jax import lax
from jax.sharding import PartitionSpec as P


def slot_numbers(route_ids, expert_count, capacity):
    token_count = route_ids.shape[0]
    onehot = (
        route_ids[:, :, None] == jnp.arange(expert_count, dtype=jnp.int32)[None, None, :]
    ).astype(jnp.int32)
    flattened = onehot.reshape(token_count * route_ids.shape[1], expert_count)
    earlier = jnp.cumsum(flattened, axis=0) - flattened
    position = jnp.sum(earlier * flattened, axis=1).reshape(route_ids.shape)
    return route_ids * capacity + position


def swiglu_backward(gate_sum, up_sum, hidden_grad):
    sigma = jax.nn.sigmoid(gate_sum)
    silu_value = gate_sum * sigma
    grad_up = (hidden_grad * silu_value).astype(jnp.bfloat16)
    grad_gate = (hidden_grad * up_sum * sigma * (1.0 + gate_sum * (1.0 - sigma))).astype(
        jnp.bfloat16
    )
    score_rows = jnp.sum(silu_value * up_sum * hidden_grad, axis=1)
    return (grad_gate, grad_up, score_rows)


def body(activations, cotangent, route_ids, gate_probs, gate_weight, up_weight, down_weight):
    expert_count = lax.axis_size("expert")
    tokens_here = route_ids.shape[0]
    capacity = min(tokens_here, 5 * tokens_here // (2 * expert_count))
    slot_total = expert_count * capacity
    destination = slot_numbers(route_ids, expert_count, capacity)
    slot_range = jnp.arange(slot_total, dtype=jnp.int32)
    matches = destination[:, :, None] == slot_range[None, None, :]
    placing = jnp.sum(matches.astype(jnp.float32), axis=1).astype(jnp.bfloat16)
    weighting = jnp.sum(jnp.where(matches, gate_probs[:, :, None], jnp.float32(0.0)), axis=1)
    gate_local = gate_weight[0]
    up_local = up_weight[0]
    down_local = down_weight[0]
    first_dims = (((0,), (0,)), ((), ()))
    down_dims = (((0,), (1,)), ((), ()))
    hidden_dims = (((1,), (1,)), ((), ()))
    send_in = jnp.dot(activations, placing, preferred_element_type=jnp.float32).astype(jnp.bfloat16)
    send_grad = jnp.dot(cotangent, placing, preferred_element_type=jnp.float32).astype(jnp.bfloat16)
    recv_in, recv_grad = (
        lax.all_to_all(send_in, "expert", split_axis=1, concat_axis=1, tiled=True),
        lax.all_to_all(send_grad, "expert", split_axis=1, concat_axis=1, tiled=True),
    )
    feature_piece = lax.all_gather(recv_in, "tensor", axis=0, tiled=True)
    grad_piece = lax.all_gather(recv_grad, "tensor", axis=0, tiled=True)
    gate_rows = gate_local
    up_rows = up_local
    gate_sum = lax.dot_general(
        feature_piece, gate_rows, first_dims, preferred_element_type=jnp.float32
    )
    up_sum = lax.dot_general(feature_piece, up_rows, first_dims, preferred_element_type=jnp.float32)
    hidden_grad = lax.dot_general(
        grad_piece, down_local, down_dims, preferred_element_type=jnp.float32
    )
    gate_sum, up_sum, hidden_grad = (gate_sum, up_sum, hidden_grad)
    grad_gate, grad_up, score_rows = swiglu_backward(gate_sum, up_sum, hidden_grad)
    gate_rows = gate_local
    up_rows = up_local
    term = lax.dot_general(gate_rows, grad_gate, hidden_dims, preferred_element_type=jnp.float32)
    term_slice = lax.psum_scatter(
        term + lax.dot_general(up_rows, grad_up, hidden_dims, preferred_element_type=jnp.float32),
        "tensor",
        scatter_dimension=0,
        tiled=True,
    )
    score_whole = lax.psum(score_rows[None, :], "tensor")
    back_terms, back_scores = (
        lax.all_to_all(term_slice, "expert", split_axis=1, concat_axis=1, tiled=True),
        lax.all_to_all(score_whole, "expert", split_axis=1, concat_axis=1, tiled=True),
    )
    grad_local = jnp.dot(
        back_terms, weighting.T, precision=lax.Precision.HIGHEST, preferred_element_type=jnp.float32
    )
    score_grad = jnp.sum(
        jnp.where(matches, back_scores[0][None, None, :], jnp.float32(0.0)), axis=2
    )
    grad_input = grad_local.astype(jnp.bfloat16)
    return (grad_input, score_grad)


def solution(mesh):
    in_specs = (
        P("tensor", "expert"),
        P("tensor", "expert"),
        P("expert", None),
        P("expert", None),
        P("expert", None, "tensor"),
        P("expert", None, "tensor"),
        P("expert", "tensor", None),
    )
    out_specs = (P("tensor", "expert"), P("expert", None))
    return jax.shard_map(body, mesh=mesh, in_specs=in_specs, out_specs=out_specs, check_vma=False)
```

profile of v0, /device:TPU:0, one launch (start us, length us, event | category | flops | bytes accessed | tf_op | source)
XLA Modules:
  0.0 196.6 jit_solution(7159178132124961180)
XLA Ops:
  7.2 0.0 copy-start
  7.2 0.0 all-gather.5.cloned.1.call-start
  7.2 0.8 copy.34
  8.0 0.1 eq.43
  8.2 0.1 eq.39
  8.3 1.2 reduce-window.6
  9.5 0.1 slice.8
  9.6 0.1 copy.36
  9.8 0.1 copy.37
  9.9 0.1 add_bitcast_fusion
  9.9 0.1 reshape.38
  10.1 0.1 copy.38
  10.2 0.7 multiply_add_fusion
  10.9 0.0 copy-done
  10.9 0.2 convolution_convert_fusion
  11.2 14.7 %all_to_all.45 = bf16[384,4,80]{0,2,1:T(8,128)(2,1)} all-to-all(bf16[384,4,80]{0,2,1:T(8,128)(2,1)S(1)} %bitcast.64), channel_id=1, replica_groups=mesh['expert'=4,'tensor'=8] {'expert'}, dimensions={1} | all-to-all | bytes 491520 | tf_op jit(solution)/shard_map/all_to_all | solution.py:48
  25.9 0.0 all-gather.5.cloned.1.call-update
  25.9 0.0 all-gather.3.cloned.1.call-start
  26.0 1.1 convolution_convert_fusion.1
  27.1 10.7 %all_to_all.46 = bf16[384,4,80]{0,2,1:T(8,128)(2,1)} all-to-all(bf16[384,4,80]{0,2,1:T(8,128)(2,1)S(1)} %bitcast.63), channel_id=1, replica_groups=mesh['expert'=4,'tensor'=8] {'expert'}, dimensions={1} | all-to-all | bytes 491520 | tf_op jit(solution)/shard_map/all_to_all | solution.py:49
  37.9 0.0 all-gather.3.cloned.1.call-update
  37.9 0.0 reduce-scatter.2.cloned.1.call-start
  37.9 14.9 %all-gather.5.cloned.1.call-done = bf16[3072,320]{0,1:T(8,128)(2,1)} async-done(((bf16[384,320]{0,1:T(8,128)(2,1)}), bf16[3072,320]{0,1:T(8,128)(2,1)}) %all-gather.5.cloned.1.call-update) | async-done | bytes 1966096 | tf_op jit(solution)/shard_map/all_gather | solution.py:51
  52.8 0.0 copy-start.2
  52.8 9.4 %fusion.2 = f32[320,2048]{1,0:T(8,128)S(1)} fusion(bf16[3072,320]{0,1:T(8,128)(2,1)} %all-gather.5.cloned.1.call-done, bf16[1,3072,2048]{2,1,0:T(8,128)(2,1)} %param.11), kind=kOutput, calls=%fused_computation.2 | convolution fusion | flops 4026531840 | bytes 17170432 | tf_op jit(solution)/shard_map/dot_general | solution.py:55
  62.2 0.0 copy-done.2
  62.2 8.9 %fusion.6 = f32[320,2048]{1,0:T(8,128)} fusion(bf16[3072,320]{0,1:T(8,128)(2,1)S(1)} %copy-done.2, bf16[1,3072,2048]{2,1,0:T(8,128)(2,1)} %param.12), kind=kOutput, calls=%fused_computation.6 | convolution fusion | flops 4026531840 | bytes 17170432 | tf_op jit(solution)/shard_map/dot_general | solution.py:58
  71.1 11.3 %all-gather.3.cloned.1.call-done = bf16[3072,320]{0,1:T(8,128)(2,1)} async-done(((bf16[384,320]{0,1:T(8,128)(2,1)}), bf16[3072,320]{0,1:T(8,128)(2,1)}) %all-gather.3.cloned.1.call-update) | async-done | bytes 1966096 | tf_op jit(solution)/shard_map/all_gather | solution.py:52
  82.3 12.0 %multiply_reduce_fusion = (f32[320]{0:T(512)S(1)}, f32[320,2048]{1,0:T(8,128)}) fusion(f32[320,2048]{1,0:T(8,128)} %fusion.6, f32[320,2048]{1,0:T(8,128)S(1)} %fusion.2, bf16[3072,320]{0,1:T(8,128)(2,1)} %all-gather.3.cloned.1.call-done, bf16[1,2048,3072]{2,1,0:T(8,128)(2,1)} %param.13), kind=kOutput, calls=%fused_computation.12 | convolution fusion | flops 4031119104 | bytes 22414592 | tf_op jit(solution)/shard_map/dot_general | solution.py:59
  94.3 12.7 %fusion = f32[320,3072]{1,0:T(8,128)} fusion(bf16[1,3072,2048]{2,1,0:T(8,128)(2,1)} %param.11, f32[320,2048]{1,0:T(8,128)S(1)} %fusion.2, f32[320,2048]{1,0:T(8,128)} %get-tuple-element.5, f32[320,2048]{1,0:T(8,128)} %fusion.6), kind=kOutput, calls=%fused_computation | convolution fusion | flops 4033085440 | bytes 24379392 | tf_op jit(solution)/shard_map/dot_general | solution.py:66
  107.0 12.6 %fusion.13 = f32[3072,320]{0,1:T(8,128)} fusion(f32[320,3072]{1,0:T(8,128)} %fusion, bf16[1,3072,2048]{2,1,0:T(8,128)(2,1)} %param.12, f32[320,2048]{1,0:T(8,128)} %get-tuple-element.5, f32[320,2048]{1,0:T(8,128)S(1)} %fusion.2), kind=kOutput, calls=%fused_computation.11 | convolution fusion | flops 4031447040 | bytes 25690112 | tf_op jit(solution)/shard_map/dot_general | solution.py:68
  119.7 0.0 copy-start.1
  119.7 0.0 reduce-scatter.2.cloned.1.call-update
  119.7 0.1 all_to_all.39
  119.8 13.1 %psum.7 = f32[1,4,80]{2,0,1:T(1,128)S(1)} all-reduce(f32[1,4,80]{2,0,1:T(1,128)S(1)} %all_to_all.39), channel_id=1, replica_groups=mesh['expert'=4,'tensor'=8] {'tensor'}, use_global_device_ids=true, to_apply=%region_7.8 | all-reduce | flops 320 | bytes 2560 | tf_op jit(solution)/shard_map/psum | solution.py:73
  132.9 9.9 %all_to_all.47 = f32[1,4,80]{2,0,1:T(1,128)S(1)} all-to-all(f32[1,4,80]{2,0,1:T(1,128)S(1)} %psum.7), channel_id=1, replica_groups=mesh['expert'=4,'tensor'=8] {'expert'}, dimensions={1} | all-to-all | bytes 2560 | tf_op jit(solution)/shard_map/all_to_all | solution.py:76
  142.8 27.1 %reduce-scatter.2.cloned.1.call-done = f32[384,320]{0,1:T(8,128)} async-done(((f32[3072,320]{0,1:T(8,128)}), f32[384,320]{0,1:T(8,128)}) %reduce-scatter.2.cloned.1.call-update) | async-done | bytes 491536 | tf_op jit(solution)/shard_map/reduce_scatter | solution.py:67
  169.9 4.6 %all-to-all-start.2 = ((f32[384,4,80]{0,2,1:T(8,128)}), f32[384,4,80]{0,2,1:T(8,128)S(1)}, u32[]{:S(2)}, u32[]{:S(2)}) async-start(f32[384,4,80]{0,2,1:T(8,128)} %bitcast.65), calls=%async_computation.3 | async-start | bytes 983040 | tf_op jit(solution)/shard_map/all_to_all | solution.py:75
  174.5 0.5 broadcast.35
  175.0 0.7 reduce.3
  175.7 0.1 broadcast_in_dim.35
  175.7 0.0 copy-done.1
  175.7 0.7 select_reduce_fusion
  176.4 11.8 %all-to-all-done.2 = f32[384,4,80]{0,2,1:T(8,128)S(1)} async-done(((f32[384,4,80]{0,2,1:T(8,128)}), f32[384,4,80]{0,2,1:T(8,128)S(1)}, u32[]{:S(2)}, u32[]{:S(2)}) %all-to-all-start.2) | async-done | bytes 491552 | tf_op jit(solution)/shard_map/all_to_all | solution.py:75
  188.3 1.8 convolution_convert_fusion.2
  (5 shorter events, 0.1 us)
Async XLA Ops:
  7.2 3.7 %copy-start = (bf16[384,128]{1,0:T(8,128)(2,1)S(1)}, bf16[384,128]{1,0:T(8,128)(2,1)}, u32[]{:S(2)}) copy-start(bf16[384,128]{1,0:T(8,128)(2,1)} %param.7) | copy-start | bytes 294916
  7.2 45.6 %all-gather.5.cloned.1.call-start = ((), (), s32[]{:S(2)}) async-start(), calls=%async_computation.6 | async-start | bytes 2211840 | tf_op jit(solution)/shard_map/all_gather | solution.py:51
  25.9 56.4 %all-gather.3.cloned.1.call-start = ((), (), s32[]{:S(2)}) async-start(), calls=%async_computation.5 | async-start | bytes 2211840 | tf_op jit(solution)/shard_map/all_gather | solution.py:52
  37.9 132.0 %reduce-scatter.2.cloned.1.call-start = ((), (), s32[]{:S(2)}) async-start(), calls=%async_computation.7 | async-start | bytes 4423680 | tf_op jit(solution)/shard_map/reduce_scatter | solution.py:67
  52.8 9.4 %copy-start.2 = (bf16[3072,320]{0,1:T(8,128)(2,1)S(1)}, bf16[3072,320]{0,1:T(8,128)(2,1)}, u32[]{:S(2)}) copy-start(bf16[3072,320]{0,1:T(8,128)(2,1)} %all-gather.5.cloned.1.call-done) | copy-start | bytes 5898244
  119.7 56.1 %copy-start.1 = (f32[128,2]{0,1:T(2,128)S(1)}, f32[128,2]{0,1:T(2,128)}, u32[]{:S(2)}) copy-start(f32[128,2]{0,1:T(2,128)} %param.10) | copy-start | bytes 3076
  169.9 18.4 %all-to-all-start.2 = ((f32[384,4,80]{0,2,1:T(8,128)}), f32[384,4,80]{0,2,1:T(8,128)S(1)}, u32[]{:S(2)}, u32[]{:S(2)}) async-start(f32[384,4,80]{0,2,1:T(8,128)} %bitcast.65), calls=%async_computation.3 | async-start | bytes 983040 | tf_op jit(solution)/shard_map/all_to_all | solution.py:75
Sparse Core Ops, SparseCore 0:
  26.1 26.7 all-gather.4
  54.7 27.6 all-gather.2
  119.8 50.0 reduce-scatter.1
where the time goes:
time: 197 us
  waiting for transfers between devices  65.1 us (33%)
  matrix products  58.7 us (30%)
  blocking collectives  48.5 us (25%)
  between operations  13.8 us (7%)
  starting transfers between devices  4.72 us (2%)
  other arithmetic  3.47 us (2%)
  local copies, waits for them, and re-layouts  2.24 us (1%)
    reduce_scatter x1, waiting for transfers between devices, body(): lax.psum_scatter(term + lax.dot_general(up_rows, grad_up, hidden_dims, pr...  27.1 us
    all_gather x1, waiting for transfers between devices, body(): feature_piece = lax.all_gather(recv_in, 'tensor', axis=0, tiled=True)  14.9 us
    all_to_all x1, blocking collectives, body(): lax.all_to_all(send_in, 'expert', split_axis=1, concat_axis=1, tiled=True)  14.7 us
    psum x1, blocking collectives, body(): score_whole = lax.psum(score_rows[None, :], 'tensor')  13.1 us
    dot_general x1, matrix products, body(): lax.dot_general(gate_rows, grad_gate, hidden_dims, preferred_element_type...  12.7 us
    dot_general x1, matrix products, body(): lax.dot_general(up_rows, grad_up, hidden_dims, preferred_element_type=jnp...  12.6 us
    dot_general x1, matrix products, body(): lax.dot_general(grad_piece, down_local, down_dims, preferred_element_type...  12 us
    all_to_all x1, waiting for transfers between devices, body(): lax.all_to_all(term_slice, 'expert', split_axis=1, concat_axis=1, tiled=T...  11.8 us
  transfers between devices with their start and end apart: 4, of which 4 were waited for; matrix products, arithmetic and copies ran while one was open for 11% of the time, Pallas kernels for 0%

commit v1 on v0

--- a/solution.py
+++ b/solution.py
@@ -2,6 +2,12 @@
 import jax.numpy as jnp
 from jax import lax
 from jax.sharding import PartitionSpec as P
+
+form_indices_here = lambda a0, local_values, across: jnp.split(
+    jax.lax.all_gather(jnp.concatenate([a0, local_values], axis=1), across, axis=0, tiled=True),
+    [a0.shape[1]],
+    1,
+)
 
 
 def slot_numbers(route_ids, expert_count, capacity):
@@ -48,8 +54,7 @@
         lax.all_to_all(send_in, "expert", split_axis=1, concat_axis=1, tiled=True),
         lax.all_to_all(send_grad, "expert", split_axis=1, concat_axis=1, tiled=True),
     )
-    feature_piece = lax.all_gather(recv_in, "tensor", axis=0, tiled=True)
-    grad_piece = lax.all_gather(recv_grad, "tensor", axis=0, tiled=True)
+    feature_piece, grad_piece = form_indices_here(recv_in, recv_grad, "tensor")
     gate_rows = gate_local
     up_rows = up_local
     gate_sum = lax.dot_general(

time: 197 us -> 206 us (1.046)
  waiting for transfers between devices: 65.1 us -> 81.9 us
  blocking collectives: 48.5 us -> 33.3 us
  starting transfers between devices: 4.72 us -> 11 us
    all_to_all x1 -> x0, blocking collectives: 14.7 us -> none  [body(): lax.all_to_all(send_in, 'expert', split_axis=1, concat_axis=1, tiled=True)]
    all_gather x2 -> x1, waiting for transfers between devices: 26.2 us -> 35.5 us  [jax.lax.all_gather(jnp.concatenate([a0, local_values], axis=1), across, a...]
    all_to_all x0 -> x1, waiting for transfers between devices: none -> 7.43 us  [body(): lax.all_to_all(send_in, 'expert', split_axis=1, concat_axis=1, tiled=True)]
    all_to_all x0 -> x1, starting transfers between devices: none -> 6.31 us  [body(): lax.all_to_all(send_in, 'expert', split_axis=1, concat_axis=1, tiled=True)]
  transfers between devices with their start and end apart: 4 -> 4, of which waited for: 4 -> 4; matrix products, arithmetic and copies ran while one was open for 11% -> 2% of each run, Pallas kernels for 0% -> 0%
where the time goes in v1:
time: 206 us; the launch traced here: 205 us
  waiting for transfers between devices  81.9 us (40%)
  matrix products  58.3 us (28%)
  blocking collectives  33.3 us (16%)
  between operations  14.1 us (7%)
  starting transfers between devices  11 us (5%)
  other arithmetic  4.29 us (2%)
  local copies, waits for them, and re-layouts  2.28 us (1%)
    all_gather x1, waiting for transfers between devices, jax.lax.all_gather(jnp.concatenate([a0, local_values], axis=1), across, a...  35.5 us
    reduce_scatter x1, waiting for transfers between devices, body(): lax.psum_scatter(term + lax.dot_general(up_rows, grad_up, hidden_dims, pr...  27.1 us
    psum x1, blocking collectives, body(): score_whole = lax.psum(score_rows[None, :], 'tensor')  13.1 us
    dot_general x1, matrix products, body(): lax.dot_general(gate_rows, grad_gate, hidden_dims, preferred_element_type...  12.7 us
    dot_general x1, matrix products, body(): lax.dot_general(up_rows, grad_up, hidden_dims, preferred_element_type=jnp...  12.6 us
    dot_general x1, matrix products, body(): lax.dot_general(grad_piece, down_local, down_dims, preferred_element_type...  12.3 us
    all_to_all x1, waiting for transfers between devices, body(): lax.all_to_all(term_slice, 'expert', split_axis=1, concat_axis=1, tiled=T...  11.8 us
    all_to_all x1, blocking collectives, body(): lax.all_to_all(send_grad, 'expert', split_axis=1, concat_axis=1, tiled=True)  10.3 us
  transfers between devices with their start and end apart: 4, of which 4 were waited for; matrix products, arithmetic and copies ran while one was open for 2% of the time, Pallas kernels for 0%

profile of v1, /device:TPU:0, one launch (start us, length us, event | category | flops | bytes accessed | tf_op | source)
XLA Modules:
  0.0 205.1 jit_solution(8976297921016044334)
XLA Ops:
  7.2 0.0 copy-start
  7.2 0.8 copy.34
  8.0 0.1 eq.43
  8.1 0.1 eq.39
  8.3 1.2 reduce-window.6
  9.5 0.1 slice.8
  9.6 0.1 copy.36
  9.7 0.1 copy.37
  9.8 0.1 add_bitcast_fusion
  9.9 0.1 reshape.38
  10.1 0.1 copy.38
  10.1 0.7 multiply_add_fusion
  10.9 0.0 copy-done
  10.9 0.9 convolution_convert_fusion.1
  11.8 6.3 %all-to-all-start = ((bf16[384,4,80]{0,2,1:T(8,128)(2,1)}), bf16[384,4,80]{0,2,1:T(8,128)(2,1)S(1)}, u32[]{:S(2)}, u32[]{:S(2)}) async-start(bf16[384,4,80]{0,2,1:T(8,128)(2,1)} %bitcast.3), calls=%async_computation | async-start | bytes 491520 | tf_op jit(solution)/shard_map/all_to_all | solution.py:54
  18.1 0.0 all-gather.2.cloned.1.call-start
  18.1 1.1 convolution_convert_fusion
  19.3 7.4 %all-to-all-done = bf16[384,4,80]{0,2,1:T(8,128)(2,1)S(1)} async-done(((bf16[384,4,80]{0,2,1:T(8,128)(2,1)}), bf16[384,4,80]{0,2,1:T(8,128)(2,1)S(1)}, u32[]{:S(2)}, u32[]{:S(2)}) %all-to-all-start) | async-done | bytes 245792 | tf_op jit(solution)/shard_map/all_to_all | solution.py:54
  26.7 10.3 %all_to_all.45 = bf16[384,4,80]{0,2,1:T(8,128)(2,1)S(1)} all-to-all(bf16[384,4,80]{0,2,1:T(8,128)(2,1)S(1)} %bitcast.58), channel_id=1, replica_groups=mesh['expert'=4,'tensor'=8] {'expert'}, dimensions={1} | all-to-all | bytes 491520 | tf_op jit(solution)/shard_map/all_to_all | solution.py:55
  37.0 0.8 pad_maximum_fusion
  37.8 0.0 all-gather.2.cloned.1.call-update
  37.8 0.0 reduce-scatter.2.cloned.1.call-start
  37.9 35.5 %all-gather.2.cloned.1.call-done = bf16[3072,640]{0,1:T(8,128)(2,1)} async-done(((bf16[384,640]{0,1:T(8,128)(2,1)}), bf16[3072,640]{0,1:T(8,128)(2,1)}) %all-gather.2.cloned.1.call-update) | async-done | bytes 3932176 | tf_op jit(solution)/shard_map/all_gather | solution.py:7
  73.4 0.0 copy-start.2
  73.4 9.4 %fusion.2 = f32[320,2048]{1,0:T(8,128)S(1)} fusion(bf16[1,3072,2048]{2,1,0:T(8,128)(2,1)} %param.11, bf16[3072,640]{0,1:T(8,128)(2,1)} %all-gather.2.cloned.1.call-done), kind=kOutput, calls=%fused_computation.2 | convolution fusion | flops 4026531840 | bytes 17170432 | tf_op jit(solution)/shard_map/dot_general | solution.py:60
  82.8 0.0 copy-done.2
  82.8 7.4 %fusion.6 = f32[320,2048]{1,0:T(8,128)S(1)} fusion(bf16[1,3072,2048]{2,1,0:T(8,128)(2,1)} %param.12, bf16[3072,640]{0,1:T(8,128)(2,1)S(1)} %copy-done.2), kind=kOutput, calls=%fused_computation.6 | convolution fusion | flops 4026531840 | bytes 17170432 | tf_op jit(solution)/shard_map/dot_general | solution.py:63
  90.3 0.0 copy-start.3
  90.3 12.3 %multiply_reduce_fusion = (f32[320]{0:T(512)S(1)}, f32[320,2048]{1,0:T(8,128)}) fusion(f32[320,2048]{1,0:T(8,128)S(1)} %fusion.6, f32[320,2048]{1,0:T(8,128)S(1)} %fusion.2, bf16[1,2048,3072]{2,1,0:T(8,128)(2,1)} %param.13, bf16[3072,640]{0,1:T(8,128)(2,1)} %all-gather.2.cloned.1.call-done), kind=kOutput, calls=%fused_computation.12 | convolution fusion | flops 4031119104 | bytes 22414592 | tf_op jit(solution)/shard_map/dot_general | solution.py:64
  102.6 0.0 copy-done.3
  102.6 12.7 %fusion = f32[320,3072]{1,0:T(8,128)} fusion(bf16[1,3072,2048]{2,1,0:T(8,128)(2,1)} %param.11, f32[320,2048]{1,0:T(8,128)S(1)} %fusion.2, f32[320,2048]{1,0:T(8,128)} %get-tuple-element.5, f32[320,2048]{1,0:T(8,128)} %copy-done.3), kind=kOutput, calls=%fused_computation | convolution fusion | flops 4033085440 | bytes 24379392 | tf_op jit(solution)/shard_map/dot_general | solution.py:71
  115.3 12.6 %fusion.13 = f32[3072,320]{0,1:T(8,128)} fusion(f32[320,3072]{1,0:T(8,128)} %fusion, bf16[1,3072,2048]{2,1,0:T(8,128)(2,1)} %param.12, f32[320,2048]{1,0:T(8,128)} %get-tuple-element.5, f32[320,2048]{1,0:T(8,128)S(1)} %fusion.2), kind=kOutput, calls=%fused_computation.11 | convolution fusion | flops 4031447040 | bytes 25690112 | tf_op jit(solution)/shard_map/dot_general | solution.py:73
  127.9 0.0 copy-start.1
  127.9 0.0 reduce-scatter.2.cloned.1.call-update
  128.0 0.1 all_to_all.39
  128.0 13.1 %psum.7 = f32[1,4,80]{2,0,1:T(1,128)S(1)} all-reduce(f32[1,4,80]{2,0,1:T(1,128)S(1)} %all_to_all.39), channel_id=1, replica_groups=mesh['expert'=4,'tensor'=8] {'tensor'}, use_global_device_ids=true, to_apply=%region_7.8 | all-reduce | flops 320 | bytes 2560 | tf_op jit(solution)/shard_map/psum | solution.py:78
  141.1 9.9 %all_to_all.46 = f32[1,4,80]{2,0,1:T(1,128)S(1)} all-to-all(f32[1,4,80]{2,0,1:T(1,128)S(1)} %psum.7), channel_id=1, replica_groups=mesh['expert'=4,'tensor'=8] {'expert'}, dimensions={1} | all-to-all | bytes 2560 | tf_op jit(solution)/shard_map/all_to_all | solution.py:81
  151.1 27.1 %reduce-scatter.2.cloned.1.call-done = f32[384,320]{0,1:T(8,128)} async-done(((f32[3072,320]{0,1:T(8,128)}), f32[384,320]{0,1:T(8,128)}) %reduce-scatter.2.cloned.1.call-update) | async-done | bytes 491536 | tf_op jit(solution)/shard_map/reduce_scatter | solution.py:72
  178.1 4.6 %all-to-all-start.2 = ((f32[384,4,80]{0,2,1:T(8,128)}), f32[384,4,80]{0,2,1:T(8,128)S(1)}, u32[]{:S(2)}, u32[]{:S(2)}) async-start(f32[384,4,80]{0,2,1:T(8,128)} %bitcast.61), calls=%async_computation.3 | async-start | bytes 983040 | tf_op jit(solution)/shard_map/all_to_all | solution.py:80
  182.7 0.5 broadcast.35
  183.2 0.7 reduce.3
  183.9 0.1 broadcast_in_dim.35
  184.0 0.0 copy-done.1
  184.0 0.7 select_reduce_fusion
  184.7 11.8 %all-to-all-done.2 = f32[384,4,80]{0,2,1:T(8,128)S(1)} async-done(((f32[384,4,80]{0,2,1:T(8,128)}), f32[384,4,80]{0,2,1:T(8,128)S(1)}, u32[]{:S(2)}, u32[]{:S(2)}) %all-to-all-start.2) | async-done | bytes 491552 | tf_op jit(solution)/shard_map/all_to_all | solution.py:80
  196.5 1.8 convolution_convert_fusion.2
  (5 shorter events, 0.1 us)
Async XLA Ops:
  7.2 3.7 %copy-start = (bf16[384,128]{1,0:T(8,128)(2,1)S(1)}, bf16[384,128]{1,0:T(8,128)(2,1)}, u32[]{:S(2)}) copy-start(bf16[384,128]{1,0:T(8,128)(2,1)} %param.7) | copy-start | bytes 294916
  11.8 14.9 %all-to-all-start = ((bf16[384,4,80]{0,2,1:T(8,128)(2,1)}), bf16[384,4,80]{0,2,1:T(8,128)(2,1)S(1)}, u32[]{:S(2)}, u32[]{:S(2)}) async-start(bf16[384,4,80]{0,2,1:T(8,128)(2,1)} %bitcast.3), calls=%async_computation | async-start | bytes 491520 | tf_op jit(solution)/shard_map/all_to_all | solution.py:54
  18.1 55.2 %all-gather.2.cloned.1.call-start = ((), (), s32[]{:S(2)}) async-start(), calls=%async_computation.5 | async-start | bytes 4423680 | tf_op jit(solution)/shard_map/all_gather | solution.py:7
  37.8 140.3 %reduce-scatter.2.cloned.1.call-start = ((), (), s32[]{:S(2)}) async-start(), calls=%async_computation.6 | async-start | bytes 4423680 | tf_op jit(solution)/shard_map/reduce_scatter | solution.py:72
  73.4 9.4 %copy-start.2 = (bf16[3072,640]{0,1:T(8,128)(2,1)S(1)}, bf16[3072,640]{0,1:T(8,128)(2,1)}, u32[]{:S(2)}) copy-start(bf16[3072,640]{0,1:T(8,128)(2,1)} %all-gather.2.cloned.1.call-done) | copy-start | bytes 11796484
  90.3 12.3 %copy-start.3 = (f32[320,2048]{1,0:T(8,128)}, f32[320,2048]{1,0:T(8,128)S(1)}, u32[]{:S(2)}) copy-start(f32[320,2048]{1,0:T(8,128)S(1)} %fusion.6) | copy-start | bytes 7864324
  127.9 56.1 %copy-start.1 = (f32[128,2]{0,1:T(2,128)S(1)}, f32[128,2]{0,1:T(2,128)}, u32[]{:S(2)}) copy-start(f32[128,2]{0,1:T(2,128)} %param.10) | copy-start | bytes 3076
  178.1 18.4 %all-to-all-start.2 = ((f32[384,4,80]{0,2,1:T(8,128)}), f32[384,4,80]{0,2,1:T(8,128)S(1)}, u32[]{:S(2)}, u32[]{:S(2)}) async-start(f32[384,4,80]{0,2,1:T(8,128)} %bitcast.61), calls=%async_computation.3 | async-start | bytes 983040 | tf_op jit(solution)/shard_map/all_to_all | solution.py:80
Sparse Core Ops, SparseCore 0:
  38.0 35.3 all-gather.1
  128.1 50.0 reduce-scatter.1
